TPU v7x, 32 devices: a whole 2x2x4 slice. The times are simulated.
32 devices in a mesh: seq: 8 (over y, x, core), exp: 4 (over z).
Axes of the slice: x: 2, y: 2, z: 4, core: 2. Of those that a mesh axis runs over, the one named last changes fastest.
Arguments:
- tokens: bfloat16 [1536, 3584], P('exp', 'seq'), may hold values from -6 to 6
- routes: int32 [1536, 2], P('exp'), may hold values from 0 to 3, all different within a row; in each aligned block of 384 rows (0 to 383, 384 to 767, ...) at most 288 rows name the same one
- damping: float32 [4, 3584], P('exp', 'seq'), may hold values from 0.1 to 1
- gate_panel: bfloat16 [4, 3584, 1024], P('exp', 'seq'), may hold values from -6 to 6
Outputs:
- whitened: bfloat16 [4, 3584, 1024], P('exp', 'seq')
Inputs may be any that keep to these rules, and one draw needn't show every extreme that they name: `routes`: each token names 2 different experts, and every expert is named by some token. Within the rows of one token shard (aligned blocks of 384 rows) no expert is named by more than 288 rows, a bound that some block reaches.
All inputs are finite; a program needn't handle non-finite values.
Results may differ from a plain program's by a relative error of at most 0.0051.
Values may be sent and summed in bfloat16 or wider, within the bound.
A program may use at most 192 MiB of HBM per device.

v0:
```python
import jax
import jax.numpy as jnp
from jax import lax
from jax.sharding import PartitionSpec as P


def spread(value, axis, root):
    mine = lax.axis_index(axis) == root
    return lax.psum(jnp.where(mine, value, jnp.zeros_like(value)), axis)


def finish_block(column, block, block_width):
    total_rows = column.shape[0]
    start_row = block * block_width
    diag_block = lax.dynamic_slice_in_dim(column, start_row, block_width, 0)
    diag_factor = jnp.linalg.cholesky(diag_block)
    identity = jnp.eye(block_width, dtype=jnp.float32)
    inverse = lax.linalg.triangular_solve(diag_factor, identity, left_side=True, lower=True)
    solved = jnp.dot(
        column, inverse.T, precision=lax.Precision.HIGHEST, preferred_element_type=jnp.float32
    )
    row_ids = jnp.arange(total_rows, dtype=jnp.int32)[:, None]
    below = row_ids >= start_row + block_width
    finished = jnp.where(below, solved, jnp.zeros_like(solved))
    return lax.dynamic_update_slice_in_dim(finished, diag_factor, start_row, 0)


def per_device(tokens, routes, damping, gate_panel):
    seq_count = lax.axis_size("seq")
    exp_count = lax.axis_size("exp")
    seq_index = lax.axis_index("seq")
    exp_index = lax.axis_index("exp")
    tok_rows, block_width = tokens.shape
    top_count = routes.shape[1]
    capacity = tok_rows * top_count * 3 // (2 * exp_count)
    total_rows = block_width * seq_count
    flat_routes = routes.reshape(-1)
    chosen = (flat_routes[:, None] == jnp.arange(exp_count, dtype=jnp.int32)[None, :]).astype(
        jnp.int32
    )
    earlier = jnp.cumsum(chosen, axis=0) - chosen
    slot_index = jnp.sum(earlier * chosen, axis=1)
    target = flat_routes * capacity + slot_index
    dispatch = jnp.arange(exp_count * capacity, dtype=jnp.int32)[:, None] == target[None, :]
    dispatch = jnp.any(dispatch.reshape(exp_count * capacity, tok_rows, top_count), axis=2).astype(
        jnp.bfloat16
    )
    local_counts = jnp.sum(chosen, axis=0).astype(jnp.float32)
    counts = lax.psum(local_counts, "exp")
    own_count = jnp.sum(jnp.where(jnp.arange(exp_count, dtype=jnp.int32) == exp_index, counts, 0.0))
    outgoing = jnp.dot(dispatch, tokens, preferred_element_type=jnp.float32).astype(jnp.bfloat16)
    arrived = lax.all_to_all(outgoing, "exp", split_axis=0, concat_axis=0, tiled=True)
    gram_block = lax.dot_general(
        lax.all_gather(arrived, "seq", axis=1, tiled=True),
        arrived,
        (((0,), (0,)), ((), ())),
        preferred_element_type=jnp.float32,
    )
    row_ids = jnp.arange(total_rows, dtype=jnp.int32)[:, None]
    col_ids = jnp.arange(block_width, dtype=jnp.int32)[None, :]
    on_diagonal = row_ids == col_ids + seq_index * block_width
    column = gram_block / own_count + jnp.where(on_diagonal, damping[0][None, :], 0.0)
    group_count = min(4, seq_count)
    per_group = seq_count // group_count
    for group in range(group_count):
        first_block = group * per_group
        row_start = first_block * block_width

        def factor_step(block, current):
            finished = finish_block(current, block, block_width)
            current = jnp.where(seq_index == block, finished, current)
            shared = spread(current[row_start:], "seq", block)
            own_rows = lax.dynamic_slice_in_dim(
                shared, seq_index * block_width - row_start, block_width, 0
            )
            correction = jnp.dot(
                shared,
                own_rows.T,
                precision=lax.Precision.HIGHEST,
                preferred_element_type=jnp.float32,
            )
            new_tail = current[row_start:] - jnp.where(seq_index > block, correction, 0.0)
            return jnp.concatenate([current[:row_start], new_tail], axis=0)

        column = lax.fori_loop(first_block, first_block + per_group, factor_step, column)
    factor_b = column.astype(jnp.bfloat16)
    result = lax.dot_general(
        factor_b,
        lax.all_gather(gate_panel[0], "seq", axis=0, tiled=True),
        (((0,), (0,)), ((), ())),
        preferred_element_type=jnp.float32,
    )
    return result.astype(jnp.bfloat16)[None]


def solution(mesh):
    in_specs = (P("exp", "seq"), P("exp", None), P("exp", "seq"), P("exp", "seq", None))
    out_specs = P("exp", "seq", None)
    return jax.shard_map(
        per_device, mesh=mesh, in_specs=in_specs, out_specs=out_specs, check_vma=False
    )
```

profile of v0, /device:TPU:0, one launch (start us, length us, event | category | flops | bytes accessed | tf_op | source)
XLA Modules:
  0.0 2280.1 jit_solution(10222308017493188460)
XLA Ops:
  12.8 34.7 %all_to_all.12 = bf16[4,288,448]{2,1,0:T(8,128)(2,1)S(1)} all-to-all(bf16[4,288,448]{2,1,0:T(8,128)(2,1)S(1)} %bitcast.381), channel_id=1, replica_groups=mesh['seq'=8,'exp'=4] {'exp'}, dimensions={0} | all-to-all | bytes 2064384 | tf_op jit(solution)/shard_map/all_to_all | solution.py:52
  60.2 41.9 %all-gather.4.cloned.1.call-done = bf16[1152,3584]{0,1:T(8,128)(2,1)} async-done(((bf16[1152,448]{0,1:T(8,128)(2,1)}), bf16[1152,3584]{0,1:T(8,128)(2,1)}) %all-gather.4.cloned.1.call-update) | async-done | bytes 8257552 | tf_op jit(solution)/shard_map/all_gather | solution.py:54
  113.7 40.3 %all-gather.6.cloned.1.call-done = bf16[1,3584,1024]{2,1,0:T(8,128)(2,1)} async-done(((bf16[1,448,1024]{2,1,0:T(8,128)(2,1)}), bf16[1,3584,1024]{2,1,0:T(8,128)(2,1)}) %all-gather.6.cloned.1.call-update) | async-done | bytes 7340048 | tf_op jit(solution)/shard_map/all_gather | solution.py:89
  154.0 574.8 %while.73 = (s32[]{:T(128)}, f32[3584,448]{0,1:T(8,128)}, s32[]{:T(128)}, s32[]{:T(128)}, s32[]{:T(128)}, /*index=5*/u32[]{:T(128)}, u32[]{:T(128)}, s32[]{:T(12...) while((s32[]{:T(128)}, f32[3584,448]{0,1:T(8,128)}, s32[]{:T(128)}, s32[]{:T(128)}, s32[]{:T(128)}, ...), condition=%wide.region_17.20_spmd, body=%wide.region_7.19_spmd.sunk | while | flops 18231418880 | bytes 122965784 | solution.py:85
  157.8 11.7 cholesky.1559
  180.1 11.7 cholesky.1562
  202.5 11.7 cholesky.1564
  245.7 39.3 %custom-call.79 = f32[4,128,128]{1,2,0:T(8,128)S(1)} custom-call(f32[4,128,128]{2,1,0:T(8,128)S(1)} %pad_maximum_fusion.14), custom_call_target="InvertDiagBlocksLowerTriangular" | custom-call | tf_op jit(solution)/shard_map/while/body/eval_jaxpr/triangular_solve/custom-call.3 | solution.py:18
  291.0 14.3 select_bitcast_fusion.20
  318.0 105.8 %all-reduce.8.cloned.1.call-done = f32[3584,448]{0,1:T(8,128)} async-done(((f32[3584,448]{0,1:T(8,128)}), f32[3584,448]{0,1:T(8,128)}) %all-reduce.8.cloned.1.call-update) | async-done | bytes 6422544 | tf_op jit(solution)/shard_map/while/body/eval_jaxpr/psum | solution.py:9
  423.8 16.7 select_subtract_fusion.8
  444.3 11.7 cholesky.1559
  466.6 11.7 cholesky.1562
  489.2 11.7 cholesky.1564
  532.2 39.3 %custom-call.79 = f32[4,128,128]{1,2,0:T(8,128)S(1)} custom-call(f32[4,128,128]{2,1,0:T(8,128)S(1)} %pad_maximum_fusion.14), custom_call_target="InvertDiagBlocksLowerTriangular" | custom-call | tf_op jit(solution)/shard_map/while/body/eval_jaxpr/triangular_solve/custom-call.3 | solution.py:18
  577.4 14.3 select_bitcast_fusion.20
  605.0 105.9 %all-reduce.8.cloned.1.call-done = f32[3584,448]{0,1:T(8,128)} async-done(((f32[3584,448]{0,1:T(8,128)}), f32[3584,448]{0,1:T(8,128)}) %all-reduce.8.cloned.1.call-update) | async-done | bytes 6422544 | tf_op jit(solution)/shard_map/while/body/eval_jaxpr/psum | solution.py:9
  710.9 16.7 select_subtract_fusion.8
  728.8 551.0 %while.75 = (s32[]{:T(128)}, f32[3584,448]{0,1:T(8,128)}, s32[]{:T(128)}, s32[]{:T(128)}, s32[]{:T(128)}, /*index=5*/s32[]{:T(128)}, s32[]{:T(128)}, s32[]{:T(12...) while((s32[]{:T(128)}, f32[3584,448]{0,1:T(8,128)}, s32[]{:T(128)}, s32[]{:T(128)}, ...), condition=%wide.region_20.23_spmd, body=%wide.region_18.22_spmd.sunk | while | flops 16071843840 | bytes 155078512 | solution.py:85
  741.0 11.7 cholesky.1616
  763.3 11.7 cholesky.1619
  785.6 11.7 cholesky.1621
  828.0 39.3 %custom-call.84 = f32[4,128,128]{1,2,0:T(8,128)S(1)} custom-call(f32[4,128,128]{2,1,0:T(8,128)S(1)} %pad_maximum_fusion.15), custom_call_target="InvertDiagBlocksLowerTriangular" | custom-call | tf_op jit(solution)/shard_map/while/body/eval_jaxpr/triangular_solve/custom-call.3 | solution.py:18
  873.2 14.3 select_bitcast_fusion.21
  902.6 88.3 %all-reduce.10.cloned.1.call-done = f32[2688,448]{0,1:T(8,128)} async-done(((f32[2688,448]{0,1:T(8,128)}), f32[2688,448]{0,1:T(8,128)}) %all-reduce.10.cloned.1.call-update) | async-done | bytes 4816912 | tf_op jit(solution)/shard_map/while/body/eval_jaxpr/psum | solution.py:9
  991.0 13.1 select_subtract_fusion.9
  1011.5 11.7 cholesky.1616
  1033.8 11.7 cholesky.1619
  1056.3 11.7 cholesky.1621
  1098.4 39.3 %custom-call.84 = f32[4,128,128]{1,2,0:T(8,128)S(1)} custom-call(f32[4,128,128]{2,1,0:T(8,128)S(1)} %pad_maximum_fusion.15), custom_call_target="InvertDiagBlocksLowerTriangular" | custom-call | tf_op jit(solution)/shard_map/while/body/eval_jaxpr/triangular_solve/custom-call.3 | solution.py:18
  1143.7 14.3 select_bitcast_fusion.21
  1173.7 88.2 %all-reduce.10.cloned.1.call-done = f32[2688,448]{0,1:T(8,128)} async-done(((f32[2688,448]{0,1:T(8,128)}), f32[2688,448]{0,1:T(8,128)}) %all-reduce.10.cloned.1.call-update) | async-done | bytes 4816912 | tf_op jit(solution)/shard_map/while/body/eval_jaxpr/psum | solution.py:9
  1261.9 13.1 select_subtract_fusion.9
  1279.8 506.6 %while.77 = (s32[]{:T(128)}, f32[3584,448]{0,1:T(8,128)}, s32[]{:T(128)}, s32[]{:T(128)}, s32[]{:T(128)}, /*index=5*/s32[]{:T(128)}, s32[]{:T(128)}, s32[]{:T(12...) while((s32[]{:T(128)}, f32[3584,448]{0,1:T(8,128)}, s32[]{:T(128)}, s32[]{:T(128)}, ...), condition=%wide.region_23.26_spmd, body=%wide.region_21.25_spmd.sunk | while | flops 13912268800 | bytes 139022160 | solution.py:85
  1292.0 11.7 cholesky.1673
  1379.6 39.3 %custom-call.89 = f32[4,128,128]{1,2,0:T(8,128)S(1)} custom-call(f32[4,128,128]{2,1,0:T(8,128)S(1)} %pad_maximum_fusion.17), custom_call_target="InvertDiagBlocksLowerTriangular" | custom-call | tf_op jit(solution)/shard_map/while/body/eval_jaxpr/triangular_solve/custom-call.3 | solution.py:18
  1424.9 14.3 select_bitcast_fusion.22
  1452.8 70.5 %all-reduce.12.cloned.1.call-done = f32[1792,448]{0,1:T(8,128)} async-done(((f32[1792,448]{0,1:T(8,128)}), f32[1792,448]{0,1:T(8,128)}) %all-reduce.12.cloned.1.call-update) | async-done | bytes 3211280 | tf_op jit(solution)/shard_map/while/body/eval_jaxpr/psum | solution.py:9
  1627.7 39.3 %custom-call.89 = f32[4,128,128]{1,2,0:T(8,128)S(1)} custom-call(f32[4,128,128]{2,1,0:T(8,128)S(1)} %pad_maximum_fusion.17), custom_call_target="InvertDiagBlocksLowerTriangular" | custom-call | tf_op jit(solution)/shard_map/while/body/eval_jaxpr/triangular_solve/custom-call.3 | solution.py:18
  1673.0 14.3 select_bitcast_fusion.22
  1701.5 70.5 %all-reduce.12.cloned.1.call-done = f32[1792,448]{0,1:T(8,128)} async-done(((f32[1792,448]{0,1:T(8,128)}), f32[1792,448]{0,1:T(8,128)}) %all-reduce.12.cloned.1.call-update) | async-done | bytes 3211280 | tf_op jit(solution)/shard_map/while/body/eval_jaxpr/psum | solution.py:9
  1786.4 476.9 %while.79 = (s32[]{:T(128)}, f32[3584,448]{0,1:T(8,128)}, s32[]{:T(128)}, s32[]{:T(128)}, s32[]{:T(128)}, /*index=5*/s32[]{:T(128)}, s32[]{:T(128)}, s32[]{:T(12...) while((s32[]{:T(128)}, f32[3584,448]{0,1:T(8,128)}, s32[]{:T(128)}, s32[]{:T(128)}, ...), condition=%wide.region_26.29_spmd, body=%wide.region_24.28_spmd.sunk | while | flops 11752693760 | bytes 129388392 | solution.py:85
  1886.1 39.3 %custom-call.94 = f32[4,128,128]{1,2,0:T(8,128)S(1)} custom-call(f32[4,128,128]{2,1,0:T(8,128)S(1)} %pad_maximum_fusion.19), custom_call_target="InvertDiagBlocksLowerTriangular" | custom-call | tf_op jit(solution)/shard_map/while/body/eval_jaxpr/triangular_solve/custom-call.3 | solution.py:18
  1931.4 14.3 select_bitcast_fusion.23
  1959.5 59.5 %all-reduce.14.cloned.1.call-done = f32[896,448]{0,1:T(8,128)} async-done(((f32[896,448]{0,1:T(8,128)}), f32[896,448]{0,1:T(8,128)}) %all-reduce.14.cloned.1.call-update) | async-done | bytes 1605648 | tf_op jit(solution)/shard_map/while/body/eval_jaxpr/psum | solution.py:9
  2119.5 39.3 %custom-call.94 = f32[4,128,128]{1,2,0:T(8,128)S(1)} custom-call(f32[4,128,128]{2,1,0:T(8,128)S(1)} %pad_maximum_fusion.19), custom_call_target="InvertDiagBlocksLowerTriangular" | custom-call | tf_op jit(solution)/shard_map/while/body/eval_jaxpr/triangular_solve/custom-call.3 | solution.py:18
  2164.8 14.3 select_bitcast_fusion.23
  2192.7 58.6 %all-reduce.14.cloned.1.call-done = f32[896,448]{0,1:T(8,128)} async-done(((f32[896,448]{0,1:T(8,128)}), f32[896,448]{0,1:T(8,128)}) %all-reduce.14.cloned.1.call-update) | async-done | bytes 1605648 | tf_op jit(solution)/shard_map/while/body/eval_jaxpr/psum | solution.py:9
  (551 shorter events, 874.8 us)
Async XLA Ops:
  6.5 4.7 copy-start
  6.5 95.6 %all-gather.4.cloned.1.call-start = ((), (), s32[]{:S(2)}) async-start(), calls=%async_computation.1 | async-start | bytes 9289728 | tf_op jit(solution)/shard_map/all_gather | solution.py:54
  7.6 94.6 %copy-start.9 = (f32[1,448]{1,0:T(1,128)S(1)}, f32[1,448]{1,0:T(1,128)}, u32[]{:S(2)}) copy-start(f32[1,448]{1,0:T(1,128)} %param.17) | copy-start | bytes 5380
  49.0 105.0 %all-gather.6.cloned.1.call-start = ((), (), s32[]{:S(2)}) async-start(), calls=%async_computation.2 | async-start | bytes 8257536 | tf_op jit(solution)/shard_map/all_gather | solution.py:89
  154.2 269.6 %all-reduce.8.cloned.1.call-start = ((), (), s32[]{:S(2)}) async-start(), calls=%async_computation.3 | async-start | bytes 12845056 | tf_op jit(solution)/shard_map/while/body/eval_jaxpr/psum | solution.py:9
  235.3 0.9 copy-start.5
  440.6 270.2 %all-reduce.8.cloned.1.call-start = ((), (), s32[]{:S(2)}) async-start(), calls=%async_computation.3 | async-start | bytes 12845056 | tf_op jit(solution)/shard_map/while/body/eval_jaxpr/psum | solution.py:9
  522.0 0.9 copy-start.5
  737.3 253.6 %all-reduce.10.cloned.1.call-start = ((), (), s32[]{:S(2)}) async-start(), calls=%async_computation.4 | async-start | bytes 9633792 | tf_op jit(solution)/shard_map/while/body/eval_jaxpr/psum | solution.py:9
  818.1 0.9 copy-start.6
  897.3 2.7 copy-start.2
  991.0 13.1 slice-start
  1007.8 254.1 %all-reduce.10.cloned.1.call-start = ((), (), s32[]{:S(2)}) async-start(), calls=%async_computation.4 | async-start | bytes 9633792 | tf_op jit(solution)/shard_map/while/body/eval_jaxpr/psum | solution.py:9
  1088.8 0.9 copy-start.6
  1168.3 2.7 copy-start.2
  1261.9 13.1 slice-start
  1288.3 234.9 %all-reduce.12.cloned.1.call-start = ((), (), s32[]{:S(2)}) async-start(), calls=%async_computation.5 | async-start | bytes 6422528 | tf_op jit(solution)/shard_map/while/body/eval_jaxpr/psum | solution.py:9
  1369.3 0.9 copy-start.7
  1449.0 3.7 copy-start.3
  1536.6 235.4 %all-reduce.12.cloned.1.call-start = ((), (), s32[]{:S(2)}) async-start(), calls=%async_computation.5 | async-start | bytes 6422528 | tf_op jit(solution)/shard_map/while/body/eval_jaxpr/psum | solution.py:9
  1617.7 0.9 copy-start.7
  1697.7 3.7 copy-start.3
  1795.0 224.0 %all-reduce.14.cloned.1.call-start = ((), (), s32[]{:S(2)}) async-start(), calls=%async_computation.6 | async-start | bytes 3211264 | tf_op jit(solution)/shard_map/while/body/eval_jaxpr/psum | solution.py:9
  1875.9 0.9 copy-start.8
  1955.4 2.7 copy-start.4
  2018.9 5.8 slice-start.1
  2028.5 222.8 %all-reduce.14.cloned.1.call-start = ((), (), s32[]{:S(2)}) async-start(), calls=%async_computation.6 | async-start | bytes 3211264 | tf_op jit(solution)/shard_map/while/body/eval_jaxpr/psum | solution.py:9
  2109.4 0.9 copy-start.8
  2188.7 2.7 copy-start.4
  2251.3 5.8 slice-start.1
  2263.3 9.4 copy-start.1
Sparse Core Ops, SparseCore 0:
  49.1 52.9 all-gather.3
  104.0 49.9 all-gather.5
  318.1 105.6 all-reduce.7
  605.1 105.7 all-reduce.7
  902.7 88.1 all-reduce.9
  1173.8 88.0 all-reduce.9
  1452.9 70.3 all-reduce.11
  1701.6 70.3 all-reduce.11
  1959.6 59.3 all-reduce.13
  2192.9 58.4 all-reduce.13
where the time goes:
time: 2290 us; the launch traced here: 2280 us
  other arithmetic  988 us (43%)
  waiting for transfers between devices  730 us (32%)
  matrix products  283 us (12%)
  local copies, waits for them, and re-layouts  161 us (7%)
  loops' own time  58.5 us (3%)
  blocking collectives  44.5 us (2%)
    psum x8, waiting for transfers between devices, spread(): return lax.psum(jnp.where(mine, value, jnp.zeros_like(value)), axis)  647 us
    another operation x112, other arithmetic, finish_block(): diag_factor = jnp.linalg.cholesky(diag_block)  583 us
    another operation x64, other arithmetic, finish_block(): lax.linalg.triangular_solve(diag_factor, identity, left_side=True, lower=...  317 us
    dot_general x8, matrix products, finish_block(): jnp.dot(column, inverse.T, precision=lax.Precision.HIGHEST, preferred_ele...  114 us
    dot_general x8, matrix products, factor_step(): jnp.dot(shared, own_rows.T, precision=lax.Precision.HIGHEST, preferred_el...  90.2 us
    another operation x88, local copies, waits for them, and re-layouts, finish_block(): lax.linalg.triangular_solve(diag_factor, identity, left_side=True, lower=...  69.6 us
    another operation x4, loops' own time, per_device(): lax.fori_loop(first_block, first_block + per_group, factor_step, column)  55.9 us
    dynamic_update_slice x8, local copies, waits for them, and re-layouts, finish_block(): return lax.dynamic_update_slice_in_dim(finished, diag_factor, start_row, 0)  48.5 us
  transfers between devices with their start and end apart: 10, of which 10 were waited for; matrix products, arithmetic and copies ran while one was open for 1% of the time, Pallas kernels for 0%

commit v1 on v0

v1 whole, which is shorter than its diff:
```python
import functools

import jax
import jax.numpy as jnp
from jax import lax
from jax.experimental import pallas as pl
from jax.experimental.pallas import tpu as pltpu
from jax.sharding import PartitionSpec as P

TILE = 256
HALF = 128
CHUNK = 4
NT = (((1,), (1,)), ((), ()))
NN = (((1,), (0,)), ((), ()))
F32 = jnp.float32
BF16 = jnp.bfloat16


def split(value):
    high = value.astype(BF16)
    return high, (value - high.astype(F32)).astype(BF16)


def mm(a, b, dims):
    return lax.dot_general(a, b, dims, preferred_element_type=F32)


def mm3(a, b, dims):
    ah, al = split(a)
    bh, bl = split(b)
    return mm(ah, bh, dims) + (mm(al, bh, dims) + mm(ah, bl, dims))


def factor_half(block):
    rows = lax.broadcasted_iota(jnp.int32, (8, HALF), 0)
    lanes = lax.broadcasted_iota(jnp.int32, (8, HALF), 1)
    count = HALF // 8
    left = [block[8 * t:8 * t + 8, :] for t in range(count)]
    right = [jnp.where(lanes == rows + 8 * t, 1.0, 0.0).astype(F32) for t in range(count)]
    for p in range(count):
        pl_, pr_ = left[p], right[p]
        cols = [jnp.broadcast_to(pl_[:, 8 * p + k:8 * p + k + 1], (8, HALF)) for k in range(8)]
        for k in range(8):
            scale = lax.rsqrt(cols[k][k:k + 1, :])
            lcol = cols[k] * scale
            ul = pl_[k:k + 1, :] * scale
            ur = pr_[k:k + 1, :] * scale
            for j in range(k + 1, 8):
                cols[j] = cols[j] - lcol * lcol[j:j + 1, :]
            below = jnp.where(rows > k, lcol, 0.0)
            pl_ = jnp.where(rows == k, ul, pl_ - below * ul)
            pr_ = jnp.where(rows == k, ur, pr_ - below * ur)
        left[p] = jnp.where(lanes >= rows + 8 * p, pl_, 0.0)
        right[p] = pr_
        if p + 1 < count:
            both = jnp.concatenate([left[p], pr_], axis=1)
            high = both.astype(BF16).astype(F32)
            low = both - high
            lhs = jnp.concatenate([high[:, :HALF], low[:, :HALF], high[:, :HALF]], axis=0)
            rhs = jnp.concatenate([high, high, low], axis=0).astype(BF16)
            update = mm(lhs.T.astype(BF16), rhs, NN)
            for t in range(p + 1, count):
                left[t] = left[t] - update[8 * t:8 * t + 8, :HALF]
                right[t] = right[t] - update[8 * t:8 * t + 8, HALF:]
    return jnp.concatenate(left, axis=0), jnp.concatenate(right, axis=0)


def factor_kernel(tiles, own_tiles, block_width, xt, damp, inv_count, out, hi, lo, acc, half, lower, inv, l21, wh, wl, sem):
    first_own = lax.axis_index("seq") * block_width // TILE

    def offset(j):
        return j * tiles - (j * (j - 1)) // 2

    def column(j, carry):
        chunks = (tiles - j + CHUNK - 1) // CHUNK
        own_x = pl.ds(pl.multiple_of(j * TILE, TILE), TILE)

        def chunk(c, inner):
            i0 = j + c * CHUNK
            for r in range(CHUNK):
                xr = jnp.minimum(i0 + r, tiles - 1)
                acc[pl.ds(r * TILE, TILE), :] = (
                    mm(xt[pl.ds(pl.multiple_of(xr * TILE, TILE), TILE), :], xt[own_x, :], NT) * inv_count[0, 0]
                )

            def earlier(k, z):
                base = offset(k)
                ah = hi[pl.ds(base + i0 - k, CHUNK)].reshape(CHUNK * TILE, TILE)
                al = lo[pl.ds(base + i0 - k, CHUNK)].reshape(CHUNK * TILE, TILE)
                bh, bl = hi[base + j - k], lo[base + j - k]
                acc[...] -= mm(ah, bh, NT) + (mm(al, bh, NT) + mm(ah, bl, NT))
                return z

            lax.fori_loop(0, j, earlier, 0)

            @pl.when(c == 0)
            def _():
                rows = lax.broadcasted_iota(jnp.int32, (TILE, TILE), 0)
                lanes = lax.broadcasted_iota(jnp.int32, (TILE, TILE), 1)
                acc[pl.ds(0, TILE), :] += jnp.where(rows == lanes, damp[j], 0.0)
                half[0] = acc[pl.ds(0, HALF), pl.ds(0, HALF)]

                def one(h, z):
                    upper, inverse = factor_half(half[h])
                    lower[h] = upper.T
                    inv[h] = inverse

                    @pl.when(h == 0)
                    def _():
                        cross = mm3(acc[pl.ds(HALF, HALF), pl.ds(0, HALF)], inverse, NT)
                        l21[...] = cross
                        half[1] = acc[pl.ds(HALF, HALF), pl.ds(HALF, HALF)] - mm3(cross, cross, NT)

                    return z

                lax.fori_loop(0, 2, one, 0)
                corner = -mm3(mm3(inv[1], l21[...], NN), inv[0], NN)
                zeros = jnp.zeros((HALF, HALF), F32)
                whole = jnp.concatenate(
                    [jnp.concatenate([inv[0], zeros], axis=1), jnp.concatenate([corner, inv[1]], axis=1)], axis=0
                )
                wh[...], wl[...] = split(whole)

            sh, sl = split(acc[...])
            solved = mm(sh, wh[...], NT) + (mm(sl, wh[...], NT) + mm(sh, wl[...], NT))
            top, rest = split(solved)
            at = pl.ds(offset(j) + c * CHUNK, CHUNK)
            hi[at] = top.reshape(CHUNK, TILE, TILE)
            lo[at] = rest.reshape(CHUNK, TILE, TILE)

            @pl.when(c == 0)
            def _():
                zeros = jnp.zeros((HALF, HALF), F32)
                whole = jnp.concatenate(
                    [jnp.concatenate([lower[0], zeros], axis=1), jnp.concatenate([l21[...], lower[1]], axis=1)], axis=0
                )
                hi[offset(j)], lo[offset(j)] = split(whole)

            return inner

        lax.fori_loop(0, chunks, chunk, 0)
        mine = j - first_own

        @pl.when((mine >= 0) & (mine < own_tiles))
        def _():
            copy = pltpu.make_async_copy(hi.at[pl.ds(offset(j), tiles)], out.at[mine, pl.ds(j, tiles)], sem)
            copy.start()
            copy.wait()

        return carry

    lax.fori_loop(0, tiles, column, 0)


def factor_columns(xt, damp, inv_count, block_width):
    total_rows, depth = xt.shape
    tiles = total_rows // TILE
    own_tiles = (block_width - 1 + TILE - 1) // TILE + 1
    room = tiles * (tiles + 1) // 2 + tiles
    vmem = pl.BlockSpec(memory_space=pltpu.VMEM)
    out = pl.pallas_call(
        functools.partial(factor_kernel, tiles, own_tiles, block_width),
        out_shape=jax.ShapeDtypeStruct((own_tiles, 2 * tiles, TILE, TILE), BF16),
        in_specs=[vmem, vmem, pl.BlockSpec(memory_space=pltpu.SMEM)],
        out_specs=pl.BlockSpec(memory_space=pl.ANY),
        scratch_shapes=[
            pltpu.VMEM((room, TILE, TILE), BF16),
            pltpu.VMEM((room, TILE, TILE), BF16),
            pltpu.VMEM((CHUNK * TILE, TILE), F32),
            pltpu.VMEM((2, HALF, HALF), F32),
            pltpu.VMEM((2, HALF, HALF), F32),
            pltpu.VMEM((2, HALF, HALF), F32),
            pltpu.VMEM((HALF, HALF), F32),
            pltpu.VMEM((TILE, TILE), BF16),
            pltpu.VMEM((TILE, TILE), BF16),
            pltpu.SemaphoreType.DMA,
        ],
        compiler_params=pltpu.CompilerParams(vmem_limit_bytes=56 * 1024 * 1024),
        cost_estimate=pl.CostEstimate(
            flops=2 * total_rows**3 + total_rows * total_rows * depth,
            bytes_accessed=2 * total_rows * (depth + own_tiles * TILE),
            transcendentals=total_rows,
        ),
    )(xt, damp.reshape(tiles, 1, TILE), inv_count.reshape(1, 1))
    return out


def per_device(tokens, routes, damping, gate_panel):
    seq_count = lax.axis_size("seq")
    exp_count = lax.axis_size("exp")
    seq_index = lax.axis_index("seq")
    exp_index = lax.axis_index("exp")
    tok_rows, block_width = tokens.shape
    top_count = routes.shape[1]
    capacity = tok_rows * top_count * 3 // (2 * exp_count)
    total_rows = block_width * seq_count
    experts = jnp.arange(exp_count, dtype=jnp.int32)
    named = jnp.any(routes[:, :, None] == experts[None, None, :], axis=1).astype(jnp.int32)
    slot = jnp.where(named > 0, jnp.cumsum(named, axis=0) - named, capacity)
    dispatch = (slot.T[:, :, None] == jnp.arange(capacity, dtype=jnp.int32)[None, None, :]).astype(BF16)
    counts = lax.psum(jnp.sum(named, axis=0).astype(F32), "exp")
    own_count = jnp.sum(jnp.where(experts == exp_index, counts, 0.0))
    outgoing = lax.dot_general(
        jnp.broadcast_to(tokens[None], (exp_count, tok_rows, block_width)), dispatch,
        (((1,), (1,)), ((0,), (0,))), preferred_element_type=F32
    ).astype(BF16)
    arrived = lax.all_to_all(outgoing, "exp", split_axis=0, concat_axis=0, tiled=True)
    own_xt = jnp.transpose(arrived, (1, 0, 2)).reshape(block_width, exp_count * capacity)
    xt = lax.all_gather(own_xt, "seq", axis=0, tiled=True)
    damp = lax.all_gather(damping[0], "seq", axis=0, tiled=True)
    panel = lax.all_gather(gate_panel[0], "seq", axis=0, tiled=True)
    out = factor_columns(xt, damp, 1.0 / own_count, block_width)
    own_tiles, tiles = out.shape[0], total_rows // TILE
    start = seq_index * block_width
    first = start // TILE * TILE
    columns = jnp.transpose(out[:, :tiles].reshape(own_tiles, total_rows, TILE), (1, 0, 2))
    columns = columns.reshape(total_rows, own_tiles * TILE)
    columns = lax.dynamic_slice_in_dim(columns, start - first, block_width, 1)
    row_ids = jnp.arange(total_rows, dtype=jnp.int32)[:, None]
    col_ids = jnp.arange(block_width, dtype=jnp.int32)[None, :] + start
    factor_b = jnp.where(row_ids >= col_ids, columns, jnp.zeros_like(columns))
    result = lax.dot_general(factor_b, panel, (((0,), (0,)), ((), ())), preferred_element_type=F32)
    return result.astype(BF16)[None]


def solution(mesh):
    in_specs = (P("exp", "seq"), P("exp", None), P("exp", "seq"), P("exp", "seq", None))
    out_specs = P("exp", "seq", None)
    return jax.shard_map(
        per_device, mesh=mesh, in_specs=in_specs, out_specs=out_specs, check_vma=False
    )
```

time: 2290 us -> 450 us (0.20)
  other arithmetic: 988 us -> 2.99 us
  waiting for transfers between devices: 730 us -> 17.1 us
  Pallas kernels: 0 us -> 321 us
  matrix products: 283 us -> 9.29 us
  local copies, waits for them, and re-layouts: 161 us -> 17.1 us
  loops' own time: 58.5 us -> 0 us
    another operation x178 -> x2, other arithmetic: 901 us -> 1.41 us  [the longest x112 583 us: finish_block(): diag_factor = jnp.linalg.cholesky(diag_block)]
    psum x8 -> x0, waiting for transfers between devices: 647 us -> none  [spread(): return lax.psum(jnp.where(mine, value, jnp.zeros_like(value)), axis)]
    pallas_call x0 -> x1, Pallas kernels: none -> 321 us  [factor_columns(): pl.pallas_call(functools.partial(factor_kernel, tiles, own_tiles, block_w...]
    dot_general x19 -> x2, matrix products: 226 us -> 9.29 us  [the longest x1 8.5 us: per_device(): lax.dot_general(factor_b, panel, (((0,), (0,)), ((), ())), preferred_elem...]
    another operation x121 -> x0, local copies, waits for them, and re-layouts: 70.8 us -> none  [the longest x88 69.6 us: finish_block(): lax.linalg.triangular_solve(diag_factor, identity, left_side=True, lower=...]
    all_gather x2, waiting for transfers between devices: 82.2 us -> 16.3 us  [the longest x1 16.3 us: per_device(): xt = lax.all_gather(own_xt, 'seq', axis=0, tiled=True)]
    another operation x12 -> x0, loops' own time: 58.5 us -> none  [the longest x4 55.9 us: per_device(): lax.fori_loop(first_block, first_block + per_group, factor_step, column)]
    another operation x104 -> x0, matrix products: 57.3 us -> none  [the longest x56 44.5 us: finish_block(): lax.linalg.triangular_solve(diag_factor, identity, left_side=True, lower=...]
  transfers between devices with their start and end apart: 10 -> 2, of which waited for: 10 -> 1; matrix products, arithmetic and copies ran while one was open for 1% -> 4% of each run, Pallas kernels for 0% -> 71%
where the time goes in v1:
time: 450 us
  Pallas kernels  321 us (71%)
  blocking collectives  67.3 us (15%)
  local copies, waits for them, and re-layouts  17.1 us (4%)
  waiting for transfers between devices  17.1 us (4%)
  between operations  14.8 us (3%)
  matrix products  9.29 us (2%)
    pallas_call x1, Pallas kernels, factor_columns(): pl.pallas_call(functools.partial(factor_kernel, tiles, own_tiles, block_w...  321 us
    all_to_all x1, blocking collectives, per_device(): lax.all_to_all(outgoing, 'exp', split_axis=0, concat_axis=0, tiled=True)  34.7 us
    unnamed x1, blocking collectives  22.8 us
    all_gather x1, waiting for transfers between devices, per_device(): xt = lax.all_gather(own_xt, 'seq', axis=0, tiled=True)  16.3 us
    psum x1, blocking collectives, per_device(): counts = lax.psum(jnp.sum(named, axis=0).astype(F32), 'exp')  9.82 us
  transfers between devices with their start and end apart: 2, of which 1 were waited for; matrix products, arithmetic and copies ran while one was open for 4% of the time, Pallas kernels for 71%

profile of v1, /device:TPU:0, one launch (start us, length us, event | category | flops | bytes accessed | tf_op | source)
XLA Modules:
  0.0 449.7 jit_solution(15129122858455076673)
XLA Ops:
  6.5 0.0 copy-start
  6.5 0.0 all-gather.5.cloned.1.call-start
  6.5 0.7 fusion.22
  7.3 1.2 reduce-window.6
  8.5 0.2 slice_reduce_fusion
  8.8 0.2 reduce-window.9
  8.9 0.1 add_bitcast_fusion
  9.0 0.0 copy-done
  9.0 0.8 fusion.14
  9.8 0.0 copy-start.2
  9.8 0.0 copy-start.1
  9.9 34.7 %all_to_all.5 = bf16[4,448,288]{1,2,0:T(8,128)(2,1)S(1)} all-to-all(bf16[4,448,288]{1,2,0:T(8,128)(2,1)S(1)} %fusion.14), channel_id=1, replica_groups=mesh['seq'=8,'exp'=4] {'exp'}, dimensions={0} | all-to-all | bytes 2064384 | tf_op jit(solution)/shard_map/all_to_all | solution.py:207
  44.5 1.6 copy.12
  46.1 0.0 all-gather.5.cloned.1.call-update
  46.1 0.0 all-gather.7.cloned.1.call-start
  46.1 0.7 all-gather.7.cloned.1.call-update
  46.8 0.1 convert_reduce_fusion
  47.0 9.8 %psum.7 = f32[4]{0:T(128)S(1)} all-reduce(f32[4]{0:T(128)S(1)} %convert_element_type.28), channel_id=1, replica_groups=mesh['seq'=8,'exp'=4] {'exp'}, use_global_device_ids=true, to_apply=%region_4.5 | all-reduce | flops 4 | bytes 32 | tf_op jit(solution)/shard_map/psum | solution.py:201
  56.8 0.0 copy-done.2
  56.8 0.6 dynamic-slice
  58.0 0.0 copy-done.1
  58.0 0.3 dynamic-update-slice
  58.3 22.8 %all-reduce = f32[3584]{0:T(1024)S(1)} all-reduce(f32[3584]{0:T(1024)S(1)} %dynamic-update-slice), channel_id=2, replica_groups=mesh['seq'=8,'exp'=4] {'seq'}, use_global_device_ids=true, to_apply=%add | all-reduce | flops 3584 | bytes 28672
  81.2 0.6 reshape.36.damp
  81.8 0.6 fusion.26
  83.1 16.3 %all-gather.5.cloned.1.call-done.xt = bf16[3584,1152]{1,0:T(8,128)(2,1)} async-done(((bf16[448,1152]{1,0:T(8,128)(2,1)}), bf16[3584,1152]{1,0:T(8,128)(2,1)}) %all-gather.5.cloned.1.call-update) | async-done | bytes 8257552 | tf_op jit(solution)/shard_map/all_gather | solution.py:209
  99.5 321.1 %shard_map.46 = bf16[3,28,256,256]{3,2,1,0:T(8,128)(2,1)} custom-call(bf16[3584,1152]{1,0:T(8,128)(2,1)} %all-gather.5.cloned.1.call-done.xt, f32[14,1,256]{2,1,0:T(1,128)} %reshape.36.damp, f32[1,1]{1,0:T(1,128)} %bitcast.7.inv_count), custom_call_target="tpu_custom_call" | custom-call | flops 106870865920 | bytes 13762560 | tf_op jit(solution)/shard_map/pallas_call | solution.py:161
  420.5 5.5 %slice.13 = bf16[3,14,256,256]{3,2,1,0:T(8,128)(2,1)} slice(bf16[3,28,256,256]{3,2,1,0:T(8,128)(2,1)} %shard_map.46), slice={[0:3], [0:14], [0:256], [0:256]} | slice | bytes 11010048 | tf_op jit(solution)/shard_map/slice | solution.py:216
  426.1 8.3 %copy.13 = bf16[3,3584,256]{1,2,0:T(8,128)(2,1)} copy(bf16[3,3584,256]{2,1,0:T(8,128)(2,1)} %bitcast.39) | data formatting | bytes 11010048 | tf_op jit(solution)/shard_map/reshape | solution.py:216
  434.3 0.0 all-gather.7.cloned.1.call-done
  434.3 8.5 %fusion.15 = bf16[1,448,1024]{2,1,0:T(8,128)(2,1)} fusion(bf16[1,3584,1024]{2,1,0:T(8,128)(2,1)} %all-gather.7.cloned.1.call-done, bf16[3584,768]{0,1:T(8,128)(2,1)} %bitcast.40, s32[]{:T(128)S(6)} %select_n.24, s32[448]{0:T(512)S(1)} %iota_add_fusion), kind=kOutput, calls=%fused_computation.12 | convolution fusion | flops 3292004352 | bytes 11470596 | tf_op jit(solution)/shard_map/dot_general | solution.py:222
  (6 shorter events, 0.0 us)
Async XLA Ops:
  6.5 2.5 copy-start
  6.5 92.9 %all-gather.5.cloned.1.call-start = ((), (), s32[]{:S(2)}) async-start(), calls=%async_computation.1 | async-start | bytes 9289728 | tf_op jit(solution)/shard_map/all_gather | solution.py:209
  9.8 47.0 %copy-start.2 = (u32[32]{0:T(128)S(1)}, u32[32]{0:T(128)}, u32[]{:S(2)}) copy-start(u32[32]{0:T(128)} %constant.49) | copy-start | bytes 388
  9.8 48.2 %copy-start.1 = (f32[1,448]{1,0:T(1,128)S(1)}, f32[1,448]{1,0:T(1,128)}, u32[]{:S(2)}) copy-start(f32[1,448]{1,0:T(1,128)} %param.6) | copy-start | bytes 5380
  46.1 388.2 %all-gather.7.cloned.1.call-start = ((), (), s32[]{:S(2)}) async-start(), calls=%async_computation.2 | async-start | bytes 8257536 | tf_op jit(solution)/shard_map/all_gather | solution.py:211
Sparse Core Ops, SparseCore 0:
  46.2 53.1 all-gather.4
  101.3 51.1 all-gather.6

commit v2 on v1

--- a/solution.py
+++ b/solution.py
@@ -143,13 +143,23 @@
 
         @pl.when((mine >= 0) & (mine < own_tiles))
         def _():
-            copy = pltpu.make_async_copy(hi.at[pl.ds(offset(j), tiles)], out.at[mine, pl.ds(j, tiles)], sem)
-            copy.start()
-            copy.wait()
+            own_copy(j, mine).start()
 
         return carry
 
+    def own_copy(j, mine):
+        return pltpu.make_async_copy(
+            hi.at[pl.ds(offset(j) - j, tiles)],
+            out.at[:, :, pl.ds(pl.multiple_of(mine * TILE, TILE), TILE)],
+            sem.at[mine],
+        )
+
     lax.fori_loop(0, tiles, column, 0)
+    for mine in range(own_tiles):
+
+        @pl.when(first_own + mine < tiles)
+        def _(mine=mine):
+            own_copy(first_own + mine, mine).wait()
 
 
 def factor_columns(xt, damp, inv_count, block_width):
@@ -160,7 +170,7 @@
     vmem = pl.BlockSpec(memory_space=pltpu.VMEM)
     out = pl.pallas_call(
         functools.partial(factor_kernel, tiles, own_tiles, block_width),
-        out_shape=jax.ShapeDtypeStruct((own_tiles, 2 * tiles, TILE, TILE), BF16),
+        out_shape=jax.ShapeDtypeStruct((tiles, TILE, own_tiles * TILE), BF16),
         in_specs=[vmem, vmem, pl.BlockSpec(memory_space=pltpu.SMEM)],
         out_specs=pl.BlockSpec(memory_space=pl.ANY),
         scratch_shapes=[
@@ -173,7 +183,7 @@
             pltpu.VMEM((HALF, HALF), F32),
             pltpu.VMEM((TILE, TILE), BF16),
             pltpu.VMEM((TILE, TILE), BF16),
-            pltpu.SemaphoreType.DMA,
+            pltpu.SemaphoreType.DMA((own_tiles,)),
         ],
         compiler_params=pltpu.CompilerParams(vmem_limit_bytes=56 * 1024 * 1024),
         cost_estimate=pl.CostEstimate(
@@ -210,17 +220,14 @@
     damp = lax.all_gather(damping[0], "seq", axis=0, tiled=True)
     panel = lax.all_gather(gate_panel[0], "seq", axis=0, tiled=True)
     out = factor_columns(xt, damp, 1.0 / own_count, block_width)
-    own_tiles, tiles = out.shape[0], total_rows // TILE
+    columns = out.reshape(total_rows, out.shape[2])
     start = seq_index * block_width
     first = start // TILE * TILE
-    columns = jnp.transpose(out[:, :tiles].reshape(own_tiles, total_rows, TILE), (1, 0, 2))
-    columns = columns.reshape(total_rows, own_tiles * TILE)
-    columns = lax.dynamic_slice_in_dim(columns, start - first, block_width, 1)
     row_ids = jnp.arange(total_rows, dtype=jnp.int32)[:, None]
-    col_ids = jnp.arange(block_width, dtype=jnp.int32)[None, :] + start
+    col_ids = jnp.arange(columns.shape[1], dtype=jnp.int32)[None, :] + first
     factor_b = jnp.where(row_ids >= col_ids, columns, jnp.zeros_like(columns))
     result = lax.dot_general(factor_b, panel, (((0,), (0,)), ((), ())), preferred_element_type=F32)
-    return result.astype(BF16)[None]
+    return lax.dynamic_slice_in_dim(result.astype(BF16), start - first, block_width, 0)[None]
 
 
 def solution(mesh):

time: 450 us -> 435 us (0.967)
  local copies, waits for them, and re-layouts: 17.1 us -> 4.22 us
    reshape x2 -> x1, local copies, waits for them, and re-layouts: 8.27 us -> 0.01 us  [the longest x1 8.26 us: per_device(): out[:, :tiles].reshape(own_tiles, total_rows, TILE)]
    slice x2 -> x1, local copies, waits for them, and re-layouts: 5.74 us -> 0.22 us  [the longest x1 5.52 us: per_device(): out[:, :tiles].reshape(own_tiles, total_rows, TILE)]
  transfers between devices with their start and end apart: 2 -> 2, of which waited for: 1 -> 1; matrix products, arithmetic and copies ran while one was open for 4% -> 1% of each run, Pallas kernels for 71% -> 73%
where the time goes in v2:
time: 435 us; the launch traced here: 434 us
  Pallas kernels  317 us (73%)
  blocking collectives  67.3 us (15%)
  waiting for transfers between devices  17.1 us (4%)
  between operations  14.8 us (3%)
  matrix products  10.6 us (2%)
    pallas_call x1, Pallas kernels, factor_columns(): pl.pallas_call(functools.partial(factor_kernel, tiles, own_tiles, block_w...  317 us
    all_to_all x1, blocking collectives, per_device(): lax.all_to_all(outgoing, 'exp', split_axis=0, concat_axis=0, tiled=True)  34.7 us
    unnamed x1, blocking collectives  22.8 us
    all_gather x1, waiting for transfers between devices, per_device(): xt = lax.all_gather(own_xt, 'seq', axis=0, tiled=True)  16.4 us
    psum x1, blocking collectives, per_device(): counts = lax.psum(jnp.sum(named, axis=0).astype(F32), 'exp')  9.82 us
    dot_general x1, matrix products, per_device(): lax.dot_general(factor_b, panel, (((0,), (0,)), ((), ())), preferred_elem...  9.81 us
  transfers between devices with their start and end apart: 2, of which 1 were waited for; matrix products, arithmetic and copies ran while one was open for 1% of the time, Pallas kernels for 73%

profile of v2, /device:TPU:0, one launch (start us, length us, event | category | flops | bytes accessed | tf_op | source)
XLA Modules:
  0.0 434.4 jit_solution(1073364993854191164)
XLA Ops:
  6.5 0.0 copy-start
  6.5 0.0 copy-start.2
  6.5 0.0 copy-start.1
  6.5 0.0 all-gather.5.cloned.1.call-start
  6.5 0.7 fusion.12
  7.3 1.2 reduce-window.6
  8.5 0.2 slice_reduce_fusion
  8.8 0.2 reduce-window.9
  8.9 0.1 add_bitcast_fusion
  9.0 0.0 copy-done
  9.0 0.8 fusion.8
  9.8 34.7 %all_to_all.5 = bf16[4,448,288]{1,2,0:T(8,128)(2,1)S(1)} all-to-all(bf16[4,448,288]{1,2,0:T(8,128)(2,1)S(1)} %fusion.8), channel_id=1, replica_groups=mesh['seq'=8,'exp'=4] {'exp'}, dimensions={0} | all-to-all | bytes 2064384 | tf_op jit(solution)/shard_map/all_to_all | solution.py:217
  44.5 1.5 copy.11
  46.0 0.0 all-gather.5.cloned.1.call-update
  46.0 0.0 all-gather.7.cloned.1.call-start
  46.1 0.7 all-gather.7.cloned.1.call-update
  46.8 0.1 convert_reduce_fusion
  46.9 9.8 %psum.7 = f32[4]{0:T(128)S(1)} all-reduce(f32[4]{0:T(128)S(1)} %convert_element_type.28), channel_id=1, replica_groups=mesh['seq'=8,'exp'=4] {'exp'}, use_global_device_ids=true, to_apply=%region_4.5 | all-reduce | flops 4 | bytes 32 | tf_op jit(solution)/shard_map/psum | solution.py:211
  56.7 0.0 copy-done.2
  56.7 0.6 dynamic-slice
  58.0 0.0 copy-done.1
  58.0 0.3 dynamic-update-slice
  58.3 22.8 %all-reduce = f32[3584]{0:T(1024)S(1)} all-reduce(f32[3584]{0:T(1024)S(1)} %dynamic-update-slice), channel_id=2, replica_groups=mesh['seq'=8,'exp'=4] {'seq'}, use_global_device_ids=true, to_apply=%add | all-reduce | flops 3584 | bytes 28672
  81.1 0.6 reshape.33.damp
  81.7 0.6 fusion.16
  83.0 16.4 %all-gather.5.cloned.1.call-done.xt = bf16[3584,1152]{1,0:T(8,128)(2,1)} async-done(((bf16[448,1152]{1,0:T(8,128)(2,1)}), bf16[3584,1152]{1,0:T(8,128)(2,1)}) %all-gather.5.cloned.1.call-update) | async-done | bytes 8257552 | tf_op jit(solution)/shard_map/all_gather | solution.py:219
  99.4 317.3 %shard_map.46 = bf16[14,256,768]{2,1,0:T(8,128)(2,1)} custom-call(bf16[3584,1152]{1,0:T(8,128)(2,1)} %all-gather.5.cloned.1.call-done.xt, f32[14,1,256]{2,1,0:T(1,128)} %reshape.33.damp, f32[1,1]{1,0:T(1,128)} %bitcast.7.inv_count), custom_call_target="tpu_custom_call" | custom-call | flops 106870865920 | bytes 13762560 | tf_op jit(solution)/shard_map/pallas_call | solution.py:171
  416.7 0.0 all-gather.7.cloned.1.call-done
  416.7 9.8 %fusion.1 = bf16[768,1024]{1,0:T(8,128)(2,1)S(1)} fusion(bf16[1,3584,1024]{2,1,0:T(8,128)(2,1)} %all-gather.7.cloned.1.call-done, bf16[3584,768]{1,0:T(8,128)(2,1)} %bitcast.35, s32[768]{0:T(1024)S(1)} %iota_add_fusion), kind=kOutput, calls=%fused_computation.2 | convolution fusion | flops 5642649600 | bytes 14420992 | tf_op jit(solution)/shard_map/dot_general | solution.py:229
  426.5 1.0 fusion.9
  (6 shorter events, 0.0 us)
Async XLA Ops:
  6.5 2.5 copy-start
  6.5 50.2 %copy-start.2 = (u32[32]{0:T(128)S(1)}, u32[32]{0:T(128)}, u32[]{:S(2)}) copy-start(u32[32]{0:T(128)} %constant.49) | copy-start | bytes 388
  6.5 51.4 %copy-start.1 = (f32[1,448]{1,0:T(1,128)S(1)}, f32[1,448]{1,0:T(1,128)}, u32[]{:S(2)}) copy-start(f32[1,448]{1,0:T(1,128)} %param.6) | copy-start | bytes 5380
  6.5 92.8 %all-gather.5.cloned.1.call-start = ((), (), s32[]{:S(2)}) async-start(), calls=%async_computation.1 | async-start | bytes 9289728 | tf_op jit(solution)/shard_map/all_gather | solution.py:219
  46.0 370.7 %all-gather.7.cloned.1.call-start = ((), (), s32[]{:S(2)}) async-start(), calls=%async_computation.2 | async-start | bytes 8257536 | tf_op jit(solution)/shard_map/all_gather | solution.py:221
Sparse Core Ops, SparseCore 0:
  46.1 53.1 all-gather.4
  101.3 50.8 all-gather.6
